TPU v7x, 512 devices: a whole 4x8x8 slice. The times are simulated.
512 devices in a mesh: row: 16 (over x, y_hi, core), col: 32 (over z, y_lo).
Axes of the slice: x: 4, y: 8 (y_hi: 2, y_lo: 4; y = y_hi * 4 + y_lo), z: 8, core: 2. Of those that a mesh axis runs over, the one named last changes fastest.
Arguments:
- block_in: bfloat16 [1024, 6144], P('col', 'row'), may hold values from -6 to 6
- block_out: bfloat16 [1024, 6144], P('col', 'row'), may hold values from -40 to 40
- hidden_pre: bfloat16 [1024, 24576], P(None, 'col'), may hold values from -6 to 6
- w_in: bfloat16 [6144, 24576], P('row', 'col'), may hold values from -0.078125 to 0.078125
- w_out: bfloat16 [24576, 6144], P('col', 'row'), may hold values from -0.0390625 to 0.0390625
- phrases: bfloat16 [512, 6144], P(None, 'row'), may hold values from -0.078125 to 0.078125
- region_ids: int32 [1024], replicated, may hold values from 0 to 511, never falling along the last dimension, each value on 1 to 4 neighbouring positions
- positive_phrase: int32 [512], replicated, may hold values from 0 to 511
Outputs:
- grad_in: bfloat16 [1024, 6144], P('col', 'row')
- grad_w_in: bfloat16 [6144, 24576], P('row', 'col')
- grad_w_out: bfloat16 [24576, 6144], P('col', 'row')
Inputs may be any that keep to these rules, and one draw needn't show every extreme that they name: `region_ids`: nondecreasing along the token dimension; each region holds 1 to 4 tokens.
All inputs are finite; a program needn't handle non-finite values.
Results may differ from a plain program's by a relative error of at most 0.007.
Values may be sent and summed in bfloat16 or wider, within the bound.
A program may use at most 64 MiB of HBM per device.

v0:
```python
import jax
import jax.numpy as jnp
from jax import lax
from jax.sharding import PartitionSpec as P

score_scale = 3.0
score_shift = -2.0
epsilon = 1e-06
half_root = 0.7071067811865476
density_norm = 0.3989422804014327


def gelu_slope(preact):
    return (
        0.5 * (1.0 + lax.erf(preact * half_root))
        + preact * jnp.exp(-0.5 * preact * preact) * density_norm
    )


def region_head(pooled, counts, phrases, positive_phrase, model_width):
    region_count = pooled.shape[0]
    phrase_count = phrases.shape[0]
    phrase_data = phrases.astype(jnp.float32)
    partial_inner = jnp.dot(
        pooled, phrase_data.T, precision=lax.Precision.HIGHEST, preferred_element_type=jnp.float32
    )
    partial_squares = jnp.sum(pooled * pooled, axis=1)
    inner, squares = lax.psum((partial_inner, partial_squares), "row")
    norms = jnp.sqrt(squares / model_width + epsilon)
    scores = inner / norms[:, None]
    phrase_range = lax.broadcasted_iota(jnp.int32, (region_count, phrase_count), 1)
    labels = jnp.where(
        phrase_range == positive_phrase[:, None], jnp.float32(1.0), jnp.float32(-1.0)
    )
    grad_scores = (
        -labels * score_scale * jax.nn.sigmoid(-labels * (score_scale * scores + score_shift))
    )
    pulled = jnp.dot(
        grad_scores,
        phrase_data,
        precision=lax.Precision.HIGHEST,
        preferred_element_type=jnp.float32,
    )
    curve = jnp.sum(grad_scores * scores, axis=1)
    grad_pooled = pulled / norms[:, None] - curve[:, None] * pooled / (
        model_width * norms[:, None] ** 2
    )
    return (grad_pooled / counts[:, None]).astype(jnp.bfloat16)


def local(block_in, block_out, hidden_pre, w_in, w_out, phrases, region_ids, positive_phrase):
    tok_local = block_in.shape[0]
    dim_block = block_in.shape[1]
    tokens_all = hidden_pre.shape[0]
    regions_all = positive_phrase.shape[0]
    model_width = dim_block * lax.axis_size("row")
    region_range = lax.broadcasted_iota(jnp.int32, (regions_all, tokens_all), 0)
    members = region_range == region_ids[None, :]
    member_table = members.astype(jnp.bfloat16)
    counts = jnp.sum(members.astype(jnp.float32), axis=1)
    pooled_sum = jnp.dot(
        member_table,
        lax.all_gather(block_out, "col", axis=0, tiled=True),
        preferred_element_type=jnp.float32,
    )
    pooled = pooled_sum / counts[:, None]
    scaled_grads = region_head(pooled, counts, phrases, positive_phrase, model_width)
    grad_out = jnp.take(scaled_grads, region_ids, axis=0)
    activated = jax.nn.gelu(hidden_pre.astype(jnp.float32), approximate=False).astype(jnp.bfloat16)
    grad_w_out = lax.dot_general(
        activated, grad_out, (((0,), (0,)), ((), ())), preferred_element_type=jnp.float32
    ).astype(jnp.bfloat16)
    partial_act = lax.dot_general(
        grad_out, w_out, (((1,), (1,)), ((), ())), preferred_element_type=jnp.float32
    )
    grad_act = lax.psum(partial_act, "row")
    grad_hidden = (grad_act * gelu_slope(hidden_pre.astype(jnp.float32))).astype(jnp.bfloat16)
    token_rows = grad_hidden
    grad_w_in = lax.dot_general(
        lax.all_gather(block_in, "col", axis=0, tiled=True),
        token_rows,
        (((0,), (0,)), ((), ())),
        preferred_element_type=jnp.float32,
    ).astype(jnp.bfloat16)
    token_rows = grad_hidden
    branch = lax.psum_scatter(
        lax.dot_general(
            token_rows, w_in, (((1,), (1,)), ((), ())), preferred_element_type=jnp.float32
        ),
        "col",
        scatter_dimension=0,
        tiled=True,
    )
    own_rows = lax.dynamic_slice_in_dim(grad_out, lax.axis_index("col") * tok_local, tok_local, 0)
    grad_in = (own_rows.astype(jnp.float32) + branch).astype(jnp.bfloat16)
    return (grad_in, grad_w_in, grad_w_out)


def solution(mesh):
    in_specs = (
        P("col", "row"),
        P("col", "row"),
        P(None, "col"),
        P("row", "col"),
        P("col", "row"),
        P(None, "row"),
        P(),
        P(),
    )
    out_specs = (P("col", "row"), P("row", "col"), P("col", "row"))
    return jax.shard_map(local, mesh=mesh, in_specs=in_specs, out_specs=out_specs, check_vma=False)
```

profile of v0, /device:TPU:2, one launch (start us, length us, event | category | flops | bytes accessed | tf_op | source)
XLA Modules:
  0.0 700.9 jit_solution(8052716827724516309)
XLA Ops:
  7.2 0.0 copy-start
  7.2 0.0 copy-start.2
  7.2 0.0 all-reduce.3.cloned.1.call-start
  7.2 1.1 convert_reduce_fusion
  8.3 92.4 %all_gather.6 = bf16[1024,384]{1,0:T(8,128)(2,1)S(1)} all-gather(bf16[32,384]{1,0:T(8,128)(2,1)} %param.9), channel_id=1, replica_groups=mesh['row'=16,'col'=32] {'col'}, dimensions={0}, use_global_device_ids=true | all-gather | bytes 811008 | tf_op jit(solution)/shard_map/all_gather | solution.py:63
  100.7 1.5 multiply_reduce_fusion.1
  102.2 0.0 copy-done.2
  102.2 2.5 fusion.82
  104.7 0.0 all-reduce.3.cloned.1.call-update
  104.7 0.0 all-reduce.5.cloned.1.call-start
  104.8 37.9 %psum.22 = f32[512]{0:T(512)S(1)} all-reduce(f32[512]{0:T(512)S(1)} %get-tuple-element.11), channel_id=1, replica_groups=mesh['row'=16,'col'=32] {'row'}, use_global_device_ids=true, to_apply=%region_3.0 | all-reduce | flops 512 | bytes 4096 | tf_op jit(solution)/shard_map/psum | solution.py:28
  142.7 0.0 copy-done.3
  142.8 133.3 %all-reduce.3.cloned.1.call-done = f32[512,512]{1,0:T(8,128)} async-done(((f32[512,512]{1,0:T(8,128)}), f32[512,512]{1,0:T(8,128)}) %all-reduce.3.cloned.1.call-update) | async-done | bytes 1048592 | tf_op jit(solution)/shard_map/psum | solution.py:28
  276.0 2.0 multiply_reduce_fusion
  278.1 2.7 fusion.49
  280.8 0.2 copy.15
  281.0 3.9 gather_fusion
  285.0 0.2 broadcast_select_fusion
  285.2 2.7 fusion.83
  287.9 0.0 all-reduce.5.cloned.1.call-update
  287.9 0.0 copy-start.1
  287.9 0.0 reduce-scatter.2.cloned.1.call-start
  288.0 225.2 %all-reduce.5.cloned.1.call-done = f32[1024,768]{1,0:T(8,128)} async-done(((f32[1024,768]{1,0:T(8,128)}), f32[1024,768]{1,0:T(8,128)}) %all-reduce.5.cloned.1.call-update) | async-done | bytes 3145744 | tf_op jit(solution)/shard_map/psum | solution.py:76
  513.1 3.0 fusion.38
  516.2 2.2 fusion.84
  518.3 0.0 reduce-scatter.2.cloned.1.call-update
  518.3 92.2 %all_gather.7 = bf16[1024,384]{1,0:T(8,128)(2,1)S(1)} all-gather(bf16[32,384]{1,0:T(8,128)(2,1)} %param.8), channel_id=1, replica_groups=mesh['row'=16,'col'=32] {'col'}, dimensions={0}, use_global_device_ids=true | all-gather | bytes 811008 | tf_op jit(solution)/shard_map/all_gather | solution.py:80
  610.5 9.3 %fusion.42 = bf16[768,384]{1,0:T(8,128)(2,1)} fusion(bf16[1024,384]{1,0:T(8,128)(2,1)S(1)} %broadcast_select_fusion, bf16[1024,768]{1,0:T(8,128)(2,1)} %param.10), kind=kOutput, calls=%fused_computation.51 | convolution fusion | flops 656179200 | bytes 2949120 | tf_op jit(solution)/shard_map/dot_general | solution.py:70
  619.8 1.0 fusion.47
  620.8 1.1 copy.16
  621.9 71.1 %reduce-scatter.2.cloned.1.call-done = f32[32,384]{1,0:T(8,128)} async-done(((f32[1024,384]{1,0:T(8,128)}), f32[32,384]{1,0:T(8,128)}) %reduce-scatter.2.cloned.1.call-update) | async-done | bytes 49168 | tf_op jit(solution)/shard_map/reduce_scatter | solution.py:86
  693.0 1.4 add_convert_fusion
  (8 shorter events, 0.0 us)
Async XLA Ops:
  7.2 278.0 %copy-start = (bf16[768,384]{1,0:T(8,128)(2,1)S(1)}, bf16[768,384]{1,0:T(8,128)(2,1)}, u32[]{:S(2)}) copy-start(bf16[768,384]{1,0:T(8,128)(2,1)} %param.12) | copy-start | bytes 1769476
  7.2 95.0 %copy-start.2 = (bf16[512,384]{1,0:T(8,128)(2,1)S(1)}, bf16[512,384]{1,0:T(8,128)(2,1)}, u32[]{:S(2)}) copy-start(bf16[512,384]{1,0:T(8,128)(2,1)} %param.13) | copy-start | bytes 1179652
  7.2 268.8 %all-reduce.3.cloned.1.call-start = ((), (), s32[]{:S(2)}) async-start(), calls=%async_computation.1 | async-start | bytes 2097152 | tf_op jit(solution)/shard_map/psum | solution.py:28
  100.7 42.0 %copy-start.3 = (s32[1024]{0:T(1024)S(1)}, s32[1024]{0:T(1024)}, u32[]{:S(2)}) copy-start(s32[1024]{0:T(1024)} %param.14) | copy-start | bytes 12292
  100.7 175.3 %copy-start.4 = (s32[512]{0:T(512)S(1)}, s32[512]{0:T(512)}, u32[]{:S(2)}) copy-start(s32[512]{0:T(512)} %param.15) | copy-start | bytes 6148
  104.7 408.4 %all-reduce.5.cloned.1.call-start = ((), (), s32[]{:S(2)}) async-start(), calls=%async_computation.2 | async-start | bytes 6291456 | tf_op jit(solution)/shard_map/psum | solution.py:76
  287.9 228.3 %copy-start.1 = (bf16[384,768]{1,0:T(8,128)(2,1)S(1)}, bf16[384,768]{1,0:T(8,128)(2,1)}, u32[]{:S(2)}) copy-start(bf16[384,768]{1,0:T(8,128)(2,1)} %param.11) | copy-start | bytes 1769476
  287.9 405.1 %reduce-scatter.2.cloned.1.call-start = ((), (), s32[]{:S(2)}) async-start(), calls=%async_computation.3 | async-start | bytes 1622016 | tf_op jit(solution)/shard_map/reduce_scatter | solution.py:86
Sparse Core Ops, SparseCore 0:
  104.9 171.1 all-reduce.2
  288.0 225.0 all-reduce.4
  518.5 174.4 reduce-scatter.1
where the time goes:
time: 701 us
  waiting for transfers between devices  430 us (61%)
  blocking collectives  223 us (32%)
  matrix products  21.8 us (3%)
  between operations  13.9 us (2%)
  other arithmetic  7.76 us (1%)
    psum x1, waiting for transfers between devices, local(): grad_act = lax.psum(partial_act, 'row')  225 us
    psum x1, waiting for transfers between devices, region_head(): inner, squares = lax.psum((partial_inner, partial_squares), 'row')  133 us
    all_gather x1, blocking collectives, local(): lax.all_gather(block_out, 'col', axis=0, tiled=True)  92.4 us
    all_gather x1, blocking collectives, local(): lax.all_gather(block_in, 'col', axis=0, tiled=True)  92.2 us
    reduce_scatter x1, waiting for transfers between devices, local(): lax.psum_scatter(lax.dot_general(token_rows, w_in, (((1,), (1,)), ((), ()...  71.1 us
    psum x1, blocking collectives, region_head(): inner, squares = lax.psum((partial_inner, partial_squares), 'row')  37.9 us
  transfers between devices with their start and end apart: 3, of which 3 were waited for; matrix products, arithmetic and copies ran while one was open for 2% of the time, Pallas kernels for 0%

commit v1 on v0

v1 whole, which is shorter than its diff:
```python
import jax
import jax.numpy as jnp
from jax import lax
from jax.experimental import pallas as pl
from jax.experimental.pallas import tpu as pltpu
from jax.sharding import PartitionSpec as P

score_scale = 3.0
score_shift = -2.0
epsilon = 1e-06
half_root = 0.7071067811865476
density_norm = 0.3989422804014327

MESH = pl.DeviceIdType.MESH
f32 = jnp.float32
bf16 = jnp.bfloat16
BLK = 32
DL = 384
FL = 768
FH = 384


def nt(a, b):
    return lax.dot_general(a, b, (((1,), (1,)), ((), ())), preferred_element_type=f32)


def nn(a, b):
    return lax.dot_general(a, b, (((1,), (0,)), ((), ())), preferred_element_type=f32)


def split3(v):
    hi = v.astype(bf16)
    rest = v - hi.astype(f32)
    mid = rest.astype(bf16)
    low = (rest - mid.astype(f32)).astype(bf16)
    return jnp.concatenate([hi, mid, low], axis=0)


def kernel(
    ids, pos, bi_own, bo_own, ph, h_any, win_any, wout_any,
    gi_out, go_out, gh_out, bi_out,
    ext, part, corebuf, xs, xr, tot, ag,
    go, bi, win, wout, hc, slope, pact, pown, pcore, pxs, pxr, ysend, yrecv, gh, pbr, rbuf,
    lsem, osem, halo_s, halo_r, cs, cr, h7s, h7r, a7s, a7r,
    bis, bir, gos, gor, pcs, pcr, pxss, pxsr, yss, ysr, gxs, gxr, gcs, gcr, rs, rr,
):
    r = lax.axis_index("row")
    c = lax.axis_index("col")
    x, yh, k = r // 4, (r // 2) % 2, r % 2
    z, yl = c // 4, c % 4
    ko = 1 - k

    def rdev(xx, yy, kk):
        return (xx * 4 + yy * 2 + kk, c)

    def cdev(cc):
        return (r, cc)

    def rcopy(src, dst, ssem, rsem, dev):
        return pltpu.make_async_remote_copy(
            src_ref=src, dst_ref=dst, send_sem=ssem, recv_sem=rsem,
            device_id=dev, device_id_type=MESH,
        )

    loads = [
        pltpu.make_async_copy(wout_any, wout, lsem.at[0]),
        pltpu.make_async_copy(win_any, win, lsem.at[1]),
        pltpu.make_async_copy(
            h_any.at[:, x, :, pl.ds(pl.multiple_of(k * FH, 128), FH)], hc, lsem.at[2]
        ),
    ]
    for cp in loads:
        cp.start()

    barrier = pltpu.get_barrier_semaphore()
    peers7 = [(dx, dy) for dx in range(4) for dy in range(2) if (dx, dy) != (0, 0)]
    rows = [rdev((x + dx) % 4, (yh + dy) % 2, k) for dx, dy in peers7]
    rows += [rdev((x + dx) % 4, yh, ko) for dx in range(4)]
    for dev in rows:
        pl.semaphore_signal(barrier, inc=1, device_id=dev, device_id_type=MESH)

    def greet(d, _):
        pl.semaphore_signal(
            barrier, inc=1, device_id=cdev((c + d) % 32), device_id_type=MESH
        )
        return 0

    lax.fori_loop(1, 32, greet, 0)
    pl.semaphore_wait(barrier, len(rows) + 31)

    right = rcopy(bo_own, ext.at[pl.ds(0, BLK)], halo_s.at[0], halo_r.at[0], cdev((c + 1) % 32))
    left = rcopy(bo_own, ext.at[pl.ds(2 * BLK, BLK)], halo_s.at[1], halo_r.at[1], cdev((c + 31) % 32))
    right.start()
    left.start()
    ext[pl.ds(BLK, BLK), :] = bo_own[...]
    ext[pl.ds(3 * BLK, BLK), :] = jnp.zeros((BLK, DL), bf16)

    lane = lax.broadcasted_iota(jnp.int32, (BLK, 128), 1)
    sub = lax.broadcasted_iota(jnp.int32, (BLK, 128), 0)

    def ids_column(b):
        line = ids[pl.ds(b // 4, 1), :].astype(f32)
        return jnp.sum(jnp.where(lane == (b % 4) * BLK + sub, line, 0.0), axis=1, keepdims=True)

    own_col = ids_column(c)
    line = jnp.where(lane[:1] >= 3 * BLK, -1.0, 0.0)
    for n, b in enumerate(((c + 31) % 32, c, (c + 1) % 32)):
        col = own_col if n == 1 else ids_column(b)
        line += jnp.sum(jnp.where(lane == n * BLK + sub, col, 0.0), axis=0, keepdims=True)
    member = jnp.where(own_col == line, 1.0, 0.0).astype(f32)
    counts = jnp.sum(member, axis=1, keepdims=True)
    pos_col = jnp.zeros((BLK, 1), f32)
    for j in range(4):
        hit = own_col == (lane + j * 128).astype(f32)
        pos_col += jnp.sum(jnp.where(hit, pos[j : j + 1, :].astype(f32), 0.0), axis=1, keepdims=True)

    right.wait()
    left.wait()
    pooled = nn(member.astype(bf16), ext[...]) / counts
    inner3 = nt(split3(pooled), ph[...])
    inner = inner3[:BLK] + (inner3[BLK : 2 * BLK] + inner3[2 * BLK :])
    squares = jnp.sum(pooled * pooled, axis=1, keepdims=True)
    for j in range(4):
        part[j] = inner[:, j * 128 : (j + 1) * 128]
    part[4] = jnp.broadcast_to(squares, (BLK, 128))

    mine = pl.ds(pl.multiple_of(k * 16, 16), 16)
    theirs = pl.ds(pl.multiple_of(ko * 16, 16), 16)
    cp = rcopy(part.at[:, theirs, :], corebuf, cs, cr, rdev(x, yh, ko))
    cp.start()
    cp.wait()
    for j in range(4):
        xs[j, 0] = part[j, mine, :] + corebuf[j]
        xs[j, 1] = part[4, mine, :] + corebuf[4]
    sends = []
    for i, (dx, dy) in enumerate(peers7):
        xx = (x + dx) % 4
        sends.append(rcopy(xs.at[xx], xr.at[i], h7s.at[i], h7r.at[i], rdev(xx, (yh + dy) % 2, k)))
    for cp in sends:
        cp.start()

    bi[c] = bi_own[...]

    def offset(i):
        half = (i + 1) // 2
        return (i % 2) * half + (1 - i % 2) * (32 - half)

    def bi_send(i, _):
        d = offset(i)
        rcopy(bi.at[c], bi.at[c], bis.at[d], bir.at[d], cdev((c + d) % 32)).start()
        return 0

    lax.fori_loop(1, 32, bi_send, 0)

    for cp in sends:
        cp.wait()
    total = xs[x]
    for i in range(7):
        total += xr[i]
    tot[...] = total
    ag[k, x] = total
    sends = []
    for i, (dx, dk) in enumerate(peers7):
        sends.append(
            rcopy(tot, ag.at[k, x], a7s.at[i], a7r.at[i], rdev((x + dx) % 4, yh, (k + dk) % 2))
        )
    for cp in sends:
        cp.start()
    for cp in sends:
        cp.wait()

    inner = jnp.concatenate(
        [jnp.concatenate([ag[kk, j, 0] for j in range(4)], axis=1) for kk in range(2)], axis=0
    )
    squares = jnp.concatenate([ag[kk, 0, 1] for kk in range(2)], axis=0)[:, :1]
    width = float(16 * DL)
    norms = jnp.sqrt(squares / width + epsilon)
    scores = inner / norms
    phrase = lax.broadcasted_iota(jnp.int32, (BLK, 512), 1).astype(f32)
    labels = jnp.where(phrase == pos_col, 1.0, -1.0).astype(f32)
    grads = -labels * score_scale * jax.nn.sigmoid(-labels * (score_scale * scores + score_shift))
    pulled3 = nn(split3(grads), ph[...])
    pulled = pulled3[:BLK] + (pulled3[BLK : 2 * BLK] + pulled3[2 * BLK :])
    curve = jnp.sum(grads * scores, axis=1, keepdims=True)
    grad_pooled = pulled / norms - curve * pooled / (width * norms * norms)
    go[yl, z] = (grad_pooled / counts).astype(bf16)

    def go_send(i, _):
        d = offset(i)
        rcopy(go.at[yl, z], go.at[yl, z], gos.at[d], gor.at[d], cdev((c + d) % 32)).start()
        return 0

    lax.fori_loop(1, 32, go_send, 0)

    for cp in loads:
        cp.wait()

    def slope_step(i, _):
        v = hc[i].astype(f32)
        slope[i] = 0.5 * (1.0 + lax.erf(v * half_root)) + v * jnp.exp(-0.5 * v * v) * density_norm
        return 0

    lax.fori_loop(0, 8, slope_step, 0)

    def go_wait(i, _):
        d = offset(i)
        src = (c + 32 - d) % 32
        slot = go.at[src % 4, src // 4]
        rcopy(slot, slot, gos.at[d], gor.at[d], cdev((c + d) % 32)).wait_recv()
        return 0

    lax.fori_loop(1, 32, go_wait, 0)
    go_outs = [pltpu.make_async_copy(go.at[q], go_out.at[:, q], osem.at[q]) for q in range(4)]
    for cp in go_outs:
        cp.start()

    def other_half(i, _):
        q = (x + 1 + i) % 4
        w = wout[pl.ds(pl.multiple_of(ko * FH, 128), FH), :]
        pact[q] = nt(go[q].reshape(8 * BLK, DL), w).astype(bf16)
        rcopy(pact.at[q], pcore.at[q], pcs.at[q], pcr.at[q], rdev(x, yh, ko)).start()
        return 0

    lax.fori_loop(0, 4, other_half, 0)

    def own_half(i, _):
        q = (x + 1 + i) % 4
        w = wout[pl.ds(pl.multiple_of(k * FH, 128), FH), :]
        pown[q] = nt(go[q].reshape(8 * BLK, DL), w)
        return 0

    lax.fori_loop(0, 4, own_half, 0)

    for i in range(3):
        q = (x + 1 + i) % 4
        rcopy(pact.at[q], pcore.at[q], pcs.at[q], pcr.at[q], rdev(x, yh, ko)).wait()
        pxs[i] = (pown[q] + pcore[q].astype(f32)).astype(bf16)
        rcopy(pxs.at[i], pxr.at[i], pxss.at[i], pxsr.at[i], rdev(q, yh, k)).start()
    rcopy(pact.at[x], pcore.at[x], pcs.at[x], pcr.at[x], rdev(x, yh, ko)).wait()
    acc = pown[x] + pcore[x].astype(f32)
    for i in range(3):
        q = (x + 1 + i) % 4
        rcopy(pxs.at[i], pxr.at[i], pxss.at[i], pxsr.at[i], rdev(q, yh, k)).wait()
        acc += pxr[i].astype(f32)
    pown[x] = acc
    ysend[...] = acc.astype(bf16)
    cp = rcopy(ysend, yrecv, yss, ysr, rdev(x, 1 - yh, k))
    cp.start()
    cp.wait()
    full = pown[x] + yrecv[...].astype(f32)
    gh[k, x] = (full * slope[...].reshape(8 * BLK, FH)).astype(bf16)

    xsends = []
    for i in range(3):
        xsends.append(
            rcopy(gh.at[k, x], gh.at[k, x], gxs.at[i], gxr.at[i], rdev((x + 1 + i) % 4, yh, k))
        )
    for cp in xsends:
        cp.start()

    def core_send(q):
        return rcopy(gh.at[k, q], gh.at[k, q], gcs.at[q], gcr.at[q], rdev(x, yh, ko))

    def core_recv(q):
        return rcopy(gh.at[ko, q], gh.at[ko, q], gcs.at[q], gcr.at[q], rdev(x, yh, ko))

    core_send(x).start()

    def branch(q):
        core_recv(q).wait_recv()
        val = nt(gh[0, q], win[:, :FH]) + nt(gh[1, q], win[:, FH:])
        pbr[q] = val.astype(bf16).reshape(8, BLK, DL)

        def scatter(j, _):
            zt = (z + j) % 8
            dst = zt * 4 + q
            d = (dst + 32 - c) % 32

            @pl.when(d != 0)
            def _():
                rcopy(pbr.at[q, zt], rbuf.at[d], rs.at[d], rr.at[d], cdev(dst)).start()

            return 0

        lax.fori_loop(0, 8, scatter, 0)

    branch(x)
    for i in range(3):
        q = (x + 3 - i) % 4
        rcopy(gh.at[k, q], gh.at[k, q], gxs.at[i], gxr.at[i], rdev((x + 1 + i) % 4, yh, k)).wait_recv()
        core_send(q).start()
        branch(q)

    gh_outs = [
        pltpu.make_async_copy(
            gh.at[kk, q], gh_out.at[kk, q], osem.at[4 + kk * 4 + q]
        )
        for kk in range(2)
        for q in range(4)
    ]
    for cp in gh_outs:
        cp.start()

    def bi_wait(i, _):
        d = offset(i)
        src = (c + 32 - d) % 32
        rcopy(bi.at[src], bi.at[src], bis.at[d], bir.at[d], cdev((c + d) % 32)).wait_recv()
        return 0

    lax.fori_loop(1, 32, bi_wait, 0)
    bi_cp = pltpu.make_async_copy(bi, bi_out, osem.at[12])
    bi_cp.start()

    pown[0, pl.ds(0, BLK), :] = go[yl, z].astype(f32) + pbr[yl, z].astype(f32)

    def collect(d, _):
        rcopy(rbuf.at[d], rbuf.at[d], rs.at[d], rr.at[d], cdev((c + d) % 32)).wait_recv()
        pown[0, pl.ds(0, BLK), :] = pown[0, pl.ds(0, BLK), :] + rbuf[d].astype(f32)
        return 0

    lax.fori_loop(1, 32, collect, 0)
    gi_out[...] = pown[0, pl.ds(0, BLK), :].astype(bf16)

    for cp in xsends:
        cp.wait_send()
    for q in range(4):
        core_send(q).wait_send()

    def drain(d, _):
        rcopy(bi.at[c], bi.at[c], bis.at[d], bir.at[d], cdev((c + d) % 32)).wait_send()
        rcopy(go.at[yl, z], go.at[yl, z], gos.at[d], gor.at[d], cdev((c + d) % 32)).wait_send()
        rcopy(pbr.at[0, 0], rbuf.at[d], rs.at[d], rr.at[d], cdev((c + d) % 32)).wait_send()
        return 0

    lax.fori_loop(1, 32, drain, 0)
    for cp in go_outs + gh_outs + [bi_cp]:
        cp.wait()


def local(block_in, block_out, hidden_pre, w_in, w_out, phrases, region_ids, positive_phrase):
    dma = pltpu.SemaphoreType.DMA
    vm = pltpu.VMEM
    vspec = pl.BlockSpec(memory_space=pltpu.VMEM)
    aspec = pl.BlockSpec(memory_space=pl.ANY)
    gi, go, gh, bi = pl.pallas_call(
        kernel,
        out_shape=(
            jax.ShapeDtypeStruct((BLK, DL), bf16),
            jax.ShapeDtypeStruct((8, 4, BLK, DL), bf16),
            jax.ShapeDtypeStruct((2, 4, 8 * BLK, FH), bf16),
            jax.ShapeDtypeStruct((32, BLK, DL), bf16),
        ),
        in_specs=[vspec] * 5 + [aspec] * 3,
        out_specs=(vspec, aspec, aspec, aspec),
        scratch_shapes=[
            vm((4 * BLK, DL), bf16),
            vm((5, BLK, 128), f32),
            vm((5, 16, 128), f32),
            vm((4, 2, 16, 128), f32),
            vm((7, 2, 16, 128), f32),
            vm((2, 16, 128), f32),
            vm((2, 4, 2, 16, 128), f32),
            vm((4, 8, BLK, DL), bf16),
            vm((32, BLK, DL), bf16),
            vm((DL, FL), bf16),
            vm((FL, DL), bf16),
            vm((8, BLK, FH), bf16),
            vm((8, BLK, FH), f32),
            vm((4, 8 * BLK, FH), bf16),
            vm((4, 8 * BLK, FH), f32),
            vm((4, 8 * BLK, FH), bf16),
            vm((3, 8 * BLK, FH), bf16),
            vm((3, 8 * BLK, FH), bf16),
            vm((8 * BLK, FH), bf16),
            vm((8 * BLK, FH), bf16),
            vm((2, 4, 8 * BLK, FH), bf16),
            vm((4, 8, BLK, DL), bf16),
            vm((32, BLK, DL), bf16),
            dma((3,)), dma((13,)), dma((2,)), dma((2,)), dma, dma, dma((7,)), dma((7,)), dma((7,)), dma((7,)),
            dma((32,)), dma((32,)), dma((32,)), dma((32,)), dma((4,)), dma((4,)), dma((3,)), dma((3,)), dma, dma,
            dma((3,)), dma((3,)), dma((4,)), dma((4,)), dma((32,)), dma((32,)),
        ],
        compiler_params=pltpu.CompilerParams(
            collective_id=0, has_side_effects=True, vmem_limit_bytes=40 * 2**20
        ),
        name="mlp_backward",
    )(
        region_ids.reshape(8, 128),
        positive_phrase.reshape(4, 128),
        block_in,
        block_out,
        phrases,
        hidden_pre.reshape(8, 4, BLK, FL),
        w_in,
        w_out,
    )
    go = go.reshape(1024, DL)
    gh = gh.reshape(2, 4, 8, BLK, FH).transpose(2, 1, 3, 0, 4).reshape(1024, FL)
    bi = bi.reshape(1024, DL)
    act = jax.nn.gelu(hidden_pre.astype(f32), approximate=False).astype(bf16)
    tn = (((0,), (0,)), ((), ()))
    grad_w_out = lax.dot_general(act, go, tn, preferred_element_type=f32).astype(bf16)
    grad_w_in = lax.dot_general(bi, gh, tn, preferred_element_type=f32).astype(bf16)
    return gi, grad_w_in, grad_w_out


def solution(mesh):
    in_specs = (
        P("col", "row"),
        P("col", "row"),
        P(None, "col"),
        P("row", "col"),
        P("col", "row"),
        P(None, "row"),
        P(),
        P(),
    )
    out_specs = (P("col", "row"), P("row", "col"), P("col", "row"))
    return jax.shard_map(local, mesh=mesh, in_specs=in_specs, out_specs=out_specs, check_vma=False)
```

time: 701 us -> 147 us (0.21)
  the two profiles are of different devices: /device:TPU:2 before, /device:TPU:9 now
where the time goes in v1:
time: 147 us; the launch traced here: 146 us
  Pallas kernels  126 us (86%)
  matrix products  9.99 us (7%)
  local copies, waits for them, and re-layouts  9.9 us (7%)
    pallas_call x1, Pallas kernels, local(): pl.pallas_call(kernel, out_shape=(jax.ShapeDtypeStruct((BLK, DL), bf16),...  126 us
    dot_general x1, matrix products, local(): lax.dot_general(act, go, tn, preferred_element_type=f32).astype(bf16)  8.36 us
    unnamed x18, local copies, waits for them, and re-layouts  8.29 us

profile of v1, /device:TPU:9, one launch (start us, length us, event | category | flops | bytes accessed | tf_op | source)
XLA Modules:
  0.0 146.2 jit_solution(8007173378701826532)
XLA Ops:
  0.6 0.0 copy-start
  0.6 1.4 copy-done
  2.0 0.0 copy-start.1
  2.0 1.1 copy-done.1
  3.1 0.0 copy-start.2
  3.1 1.1 copy-done.2
  4.2 0.0 copy-start.3
  4.2 1.0 copy-done.3
  5.2 0.0 copy-start.4
  5.2 0.7 copy-done.4
  5.9 0.0 copy-start.5
  5.9 0.7 copy-done.5
  6.6 0.0 copy-start.6
  6.6 0.7 copy-done.6
  7.3 0.0 copy-start.7
  7.3 0.7 copy-done.7
  8.0 125.6 %mlp_backward.1 = (bf16[32,384]{1,0:T(8,128)(2,1)S(1)}, bf16[8,4,32,384]{3,2,1,0:T(8,128)(2,1)S(1)}, bf16[2,4,256,384]{3,2,1,0:T(8,128)(2,1)S(1)}, bf16[32,32,384]{2,1,0:T(8,128)(2,1)S(1)}) custom-call(s32[8,128]{1,0:T(8,128)S(1)} %bitcast.16, s32[4,128]{1,0:T(4,128)S(1)} %bitcast.17, bf16[32,384]{1,0:T(8,128)(2,1)S(1)} %copy-done.4, ...), custom_call_target="tpu_custom_call" | custom-call | tf_op jit(solution)/shard_map/mlp_backward/pallas_call | solution.py:345
  133.6 8.4 %fusion.33 = bf16[768,384]{1,0:T(8,128)(2,1)} fusion(bf16[1024,384]{1,0:T(8,128)(2,1)S(1)} %bitcast.18, bf16[1024,768]{1,0:T(8,128)(2,1)S(1)} %copy-done), kind=kOutput, calls=%fused_computation.35 | convolution fusion | flops 656179200 | bytes 2949120 | tf_op jit(solution)/shard_map/dot_general | solution.py:402
  142.0 1.6 %copy.11 = bf16[2,4,8,32,384]{4,0,3,1,2:T(2,128)(2,1)S(1)} copy(bf16[2,4,8,32,384]{4,3,2,1,0:T(8,128)(2,1)S(1)} %bitcast.13) | data formatting | bytes 3145728 | tf_op jit(solution)/shard_map/reshape | solution.py:398
  143.6 0.3 copy.12
  143.9 1.6 %convolution_convert_fusion = bf16[384,768]{1,0:T(8,128)(2,1)} fusion(bf16[1024,384]{1,0:T(8,128)(2,1)S(1)} %bitcast.15, bf16[1024,768]{1,0:T(8,128)(2,1)S(1)} %bitcast.19), kind=kOutput, calls=%fused_computation.36 | convolution fusion | flops 604274688 | bytes 2949120 | tf_op jit(solution)/shard_map/dot_general | solution.py:403
  145.6 0.6 copy.14
Async XLA Ops:
  0.6 1.4 copy-start
  2.0 1.1 copy-start.1
  3.1 1.1 copy-start.2
  4.2 1.0 copy-start.3
  5.2 0.7 copy-start.4
  5.9 0.7 copy-start.5
  6.6 0.7 copy-start.6
  7.3 0.7 copy-start.7

commit v2 on v1

v2 whole, which is shorter than its diff:
```python
import jax
import jax.numpy as jnp
from jax import lax
from jax.experimental import pallas as pl
from jax.experimental.pallas import tpu as pltpu
from jax.sharding import PartitionSpec as P

score_scale = 3.0
score_shift = -2.0
epsilon = 1e-06
half_root = 0.7071067811865476
density_norm = 0.3989422804014327

MESH = pl.DeviceIdType.MESH
f32 = jnp.float32
bf16 = jnp.bfloat16
BLK = 32
DL = 384
FL = 768
FH = 384


GROUPS = 4


def away(place):
    return (place % 2) * ((place + 1) // 2) + (1 - place % 2) * (8 - place // 2)


def nt(a, b):
    return lax.dot_general(a, b, (((1,), (1,)), ((), ())), preferred_element_type=f32)


def nn(a, b):
    return lax.dot_general(a, b, (((1,), (0,)), ((), ())), preferred_element_type=f32)


def tn(a, b):
    return lax.dot_general(a, b, (((0,), (0,)), ((), ())), preferred_element_type=f32)


def split3(v):
    hi = v.astype(bf16)
    rest = v - hi.astype(f32)
    mid = rest.astype(bf16)
    low = (rest - mid.astype(f32)).astype(bf16)
    return jnp.concatenate([hi, mid, low], axis=0)


def kernel(
    ids, pos, bi_own, bo_hbm, ph_hbm, h_hbm, win_hbm, wout_hbm,
    gi_out, dwin_out, dwout_out,
    bo_own, ph, ext, part, corebuf, xs, xr, tot, ag,
    go, bi, win, wout, hv, act, slope, dwout, dwin, dwout_b, dwin_b, pact, pown, pcore, acc, pxs, pxr, ysend, yrecv, gh, pbr, rbuf, gsum,
    lsem, osem, halo_s, halo_r, cs, cr, h7s, h7r, a7s, a7r,
    bis, bir, gos, gor, pcs, pcr, pxss, pxsr, yss, ysr, gxs, gxr, gcs, gcr, rs, rr,
):
    r = lax.axis_index("row")
    c = lax.axis_index("col")
    x, yh, k = r // 4, (r // 2) % 2, r % 2
    z, yl = c // 4, c % 4
    ko = 1 - k

    def rdev(xx, yy, kk):
        return (xx * 4 + yy * 2 + kk, c)

    def cdev(cc):
        return (r, cc)

    def rcopy(src, dst, ssem, rsem, dev):
        return pltpu.make_async_remote_copy(
            src_ref=src, dst_ref=dst, send_sem=ssem, recv_sem=rsem,
            device_id=dev, device_id_type=MESH,
        )

    loads = [
        pltpu.make_async_copy(src, dst, lsem.at[n])
        for n, (src, dst) in enumerate(
            ((bo_hbm, bo_own), (bi_own, bi.at[0, yl, 0]), (ph_hbm, ph), (wout_hbm, wout), (win_hbm, win))
        )
    ]
    loads += [
        pltpu.make_async_copy(
            h_hbm.at[(z + away(p)) % 8], hv.at[p // 2, :, p % 2], lsem.at[5 + p]
        )
        for p in range(8)
    ]
    for cp in loads:
        cp.start()

    barrier = pltpu.get_barrier_semaphore()
    peers7 = [(dx, dy) for dx in range(4) for dy in range(2) if (dx, dy) != (0, 0)]
    rows = [rdev((x + dx) % 4, (yh + dy) % 2, k) for dx, dy in peers7]
    rows += [rdev((x + dx) % 4, yh, ko) for dx in range(4)]
    for dev in rows:
        pl.semaphore_signal(barrier, inc=1, device_id=dev, device_id_type=MESH)

    def greet(d, _):
        pl.semaphore_signal(
            barrier, inc=1, device_id=cdev((c + d) % 32), device_id_type=MESH
        )
        return 0

    lax.fori_loop(1, 32, greet, 0)
    pl.semaphore_wait(barrier, len(rows) + 31)

    for cp in loads[:2]:
        cp.wait()

    right = rcopy(bo_own, ext.at[pl.ds(0, BLK)], halo_s.at[0], halo_r.at[0], cdev((c + 1) % 32))
    left = rcopy(bo_own, ext.at[pl.ds(2 * BLK, BLK)], halo_s.at[1], halo_r.at[1], cdev((c + 31) % 32))
    right.start()
    left.start()
    ext[pl.ds(BLK, BLK), :] = bo_own[...]
    ext[pl.ds(3 * BLK, BLK), :] = jnp.zeros((BLK, DL), bf16)

    def spread(buf, send, recv, n):
        place, to = n // 4, n % 4
        dev = cdev(((z + 8 - away(place)) % 8) * 4 + to)
        return rcopy(buf.at[0, yl, 0], buf.at[place // 2, yl, place % 2], send.at[n], recv.at[place * 4 + yl], dev)

    def landed(buf, send, recv, n):
        place, of = n // 4, n % 4
        slot = buf.at[place // 2, of, place % 2]
        return rcopy(slot, slot, send.at[n], recv.at[n], cdev(((z + away(place)) % 8) * 4 + of))

    def each(lo, hi, step):
        def body(n, _):
            @pl.when(n != yl)
            def _():
                step(n)

            return 0

        lax.fori_loop(4 * lo, 4 * hi, body, 0)

    each(0, 8, lambda n: spread(bi, bis, bir, n).start())

    lane = lax.broadcasted_iota(jnp.int32, (BLK, 128), 1)
    sub = lax.broadcasted_iota(jnp.int32, (BLK, 128), 0)

    def ids_column(b):
        line = ids[pl.ds(b // 4, 1), :].astype(f32)
        return jnp.sum(jnp.where(lane == (b % 4) * BLK + sub, line, 0.0), axis=1, keepdims=True)

    own_col = ids_column(c)
    line = jnp.where(lane[:1] >= 3 * BLK, -1.0, 0.0)
    for n, b in enumerate(((c + 31) % 32, c, (c + 1) % 32)):
        col = own_col if n == 1 else ids_column(b)
        line += jnp.sum(jnp.where(lane == n * BLK + sub, col, 0.0), axis=0, keepdims=True)
    member = jnp.where(own_col == line, 1.0, 0.0).astype(f32)
    counts = jnp.sum(member, axis=1, keepdims=True)
    pos_col = jnp.zeros((BLK, 1), f32)
    for j in range(4):
        hit = own_col == (lane + j * 128).astype(f32)
        pos_col += jnp.sum(jnp.where(hit, pos[j : j + 1, :].astype(f32), 0.0), axis=1, keepdims=True)

    loads[2].wait()
    right.wait()
    left.wait()
    pooled = nn(member.astype(bf16), ext[...]) / counts
    inner3 = nt(split3(pooled), ph[...])
    inner = inner3[:BLK] + (inner3[BLK : 2 * BLK] + inner3[2 * BLK :])
    squares = jnp.sum(pooled * pooled, axis=1, keepdims=True)
    for j in range(4):
        part[j] = inner[:, j * 128 : (j + 1) * 128]
    part[4] = jnp.broadcast_to(squares, (BLK, 128))

    mine = pl.ds(pl.multiple_of(k * 16, 16), 16)
    theirs = pl.ds(pl.multiple_of(ko * 16, 16), 16)
    cp = rcopy(part.at[:, theirs, :], corebuf, cs, cr, rdev(x, yh, ko))
    cp.start()
    cp.wait()
    for j in range(4):
        xs[j, 0] = part[j, mine, :] + corebuf[j]
        xs[j, 1] = part[4, mine, :] + corebuf[4]
    sends = []
    for i, (dx, dy) in enumerate(peers7):
        xx = (x + dx) % 4
        sends.append(rcopy(xs.at[xx], xr.at[i], h7s.at[i], h7r.at[i], rdev(xx, (yh + dy) % 2, k)))
    for cp in sends:
        cp.start()


    for cp in loads[5:]:
        cp.wait()

    def act_step(n, _):
        g, q, i = n // 8, (n // 2) % 4, n % 2
        v = hv[g, q, i].astype(f32)
        act[g, q, i] = (0.5 * v * (1.0 + lax.erf(v * half_root))).astype(bf16)
        return 0

    lax.fori_loop(0, 16, act_step, 0)

    for cp in sends:
        cp.wait()
    total = xs[x]
    for i in range(7):
        total += xr[i]
    tot[...] = total
    ag[k, x] = total
    sends = []
    for i, (dx, dk) in enumerate(peers7):
        sends.append(
            rcopy(tot, ag.at[k, x], a7s.at[i], a7r.at[i], rdev((x + dx) % 4, yh, (k + dk) % 2))
        )
    for cp in sends:
        cp.start()

    lax.fori_loop(16, 32, act_step, 0)

    def slope_step(n, _):
        v = hv[n // 2, x, n % 2, :, pl.ds(pl.multiple_of(k * FH, 128), FH)].astype(f32)
        slope[n] = 0.5 * (1.0 + lax.erf(v * half_root)) + v * jnp.exp(-0.5 * v * v) * density_norm
        return 0

    lax.fori_loop(0, 8, slope_step, 0)

    for cp in sends:
        cp.wait()

    inner = jnp.concatenate(
        [jnp.concatenate([ag[kk, j, 0] for j in range(4)], axis=1) for kk in range(2)], axis=0
    )
    squares = jnp.concatenate([ag[kk, 0, 1] for kk in range(2)], axis=0)[:, :1]
    width = float(16 * DL)
    norms = jnp.sqrt(squares / width + epsilon)
    scores = inner / norms
    phrase = lax.broadcasted_iota(jnp.int32, (BLK, 512), 1).astype(f32)
    labels = jnp.where(phrase == pos_col, 1.0, -1.0).astype(f32)
    grads = -labels * score_scale * jax.nn.sigmoid(-labels * (score_scale * scores + score_shift))
    pulled3 = nn(split3(grads), ph[...])
    pulled = pulled3[:BLK] + (pulled3[BLK : 2 * BLK] + pulled3[2 * BLK :])
    curve = jnp.sum(grads * scores, axis=1, keepdims=True)
    grad_pooled = pulled / norms - curve * pooled / (width * norms * norms)
    go[0, yl, 0] = (grad_pooled / counts).astype(bf16)

    each(0, 8, lambda n: spread(go, gos, gor, n).start())

    for cp in loads[3:5]:
        cp.wait()

    whalf = [wout.at[pl.ds(pl.multiple_of(kk * FH, 128), FH), :] for kk in (ko, k)]

    def core_sum(g):
        return rcopy(pact.at[g], pcore.at[g], pcs.at[g], pcr.at[g], rdev(x, yh, ko))

    def x_sum(g, i):
        n = g * 3 + i
        return rcopy(pxs.at[n], pxr.at[n], pxss.at[n], pxsr.at[n], rdev((x + 1 + i) % 4, yh, k))

    def y_sum(g):
        return rcopy(ysend.at[g], yrecv.at[g], yss.at[g], ysr.at[g], rdev(x, 1 - yh, k))

    def x_back(g, i):
        slot = gh.at[k, g, x]
        return rcopy(slot, slot, gxs.at[g * 3 + i], gxr.at[g * 3 + i], rdev((x + 1 + i) % 4, yh, k))

    def x_backed(g, i):
        slot = gh.at[k, g, (x + 3 - i) % 4]
        return rcopy(slot, slot, gxs.at[g * 3 + i], gxr.at[g * 3 + i], rdev((x + 1 + i) % 4, yh, k))

    def core_back(g, q, kk):
        slot = gh.at[kk, g, q]
        return rcopy(slot, slot, gcs.at[g * 4 + q], gcr.at[g * 4 + q], rdev(x, yh, ko))

    def term(n):
        place, to = n // 4, n % 4
        dev = cdev(((z + away(place)) % 8) * 4 + to)
        return rcopy(pbr.at[place // 2, to, place % 2], rbuf.at[place * 4 + yl], rs.at[n], rr.at[place * 4 + yl], dev)

    def product(g):
        each(2 * g, 2 * g + 2, lambda n: landed(go, gos, gor, n).wait_recv())
        a = go[g].reshape(8 * BLK, DL)
        pact[g] = nt(a, whalf[0][...]).astype(bf16).reshape(4, 2, BLK, FH)
        core_sum(g).start()
        pown[g] = nt(a, whalf[1][...]).reshape(4, 2, BLK, FH)

    def to_x(g):
        core_sum(g).wait()
        for i in range(3):
            q = (x + 1 + i) % 4
            pxs[g * 3 + i] = (pown[g, q] + pcore[g, q].astype(f32)).astype(bf16)
            x_sum(g, i).start()
        acc[g] = pown[g, x] + pcore[g, x].astype(f32)

    def to_y(g):
        for i in range(3):
            x_sum(g, i).wait()
        val = acc[g]
        for i in range(3):
            val += pxr[g * 3 + i].astype(f32)
        acc[g] = val
        ysend[g] = val.astype(bf16)
        y_sum(g).start()

    def hidden(g):
        y_sum(g).wait()
        full = acc[g] + yrecv[g].astype(f32)
        gh[k, g, x] = (full * slope[2 * g : 2 * g + 2]).astype(bf16)
        for i in range(3):
            x_back(g, i).start()
        core_back(g, x, k).start()

    def forward(g):
        for i in range(3):
            x_backed(g, i).wait_recv()
            core_back(g, (x + 3 - i) % 4, k).start()

    def branch(g):
        for q in range(4):
            core_back(g, q, ko).wait_recv()
        val = nt(gh[0, g].reshape(8 * BLK, FH), win[:, :FH]) + nt(gh[1, g].reshape(8 * BLK, FH), win[:, FH:])
        pbr[g] = val.astype(bf16).reshape(4, 2, BLK, DL)
        each(2 * g, 2 * g + 2, lambda n: term(n).start())

    def weight_out(g):
        val = tn(act[g].reshape(8 * BLK, FL), go[g].reshape(8 * BLK, DL))
        if g:
            val += dwout[...]
        if g < GROUPS - 1:
            dwout[...] = val
        else:
            dwout_b[...] = val.astype(bf16)
            dwout_cp.start()

    def weight_in(g):
        for kk in range(2):
            val = tn(bi[g].reshape(8 * BLK, DL), gh[kk, g].reshape(8 * BLK, FH))
            if g:
                val += dwin[kk]
            if g < GROUPS - 1:
                dwin[kk] = val
            else:
                dwin_b[:, kk * FH : (kk + 1) * FH] = val.astype(bf16)
        if g == GROUPS - 1:
            dwin_cp.start()

    dwout_cp = pltpu.make_async_copy(dwout_b, dwout_out, osem.at[0])
    dwin_cp = pltpu.make_async_copy(dwin_b, dwin_out, osem.at[1])

    steps = (branch, forward, hidden, to_y, to_x, product)
    for t in range(GROUPS + len(steps) - 1):
        for late, step in enumerate(steps):
            g = t - (len(steps) - 1 - late)
            if 0 <= g < GROUPS:
                step(g)
        if 0 <= t - 1 < GROUPS:
            weight_out(t - 1)
        if t == GROUPS:
            each(0, 8, lambda n: landed(bi, bis, bir, n).wait_recv())
        if 0 <= t - 5 < GROUPS:
            weight_in(t - 5)

    gsum[...] = go[0, yl, 0].astype(f32) + pbr[0, yl, 0].astype(f32)

    def collect(n):
        slot = rbuf.at[n]
        rcopy(slot, slot, rs.at[n], rr.at[n], cdev((c + 1) % 32)).wait_recv()
        gsum[...] += rbuf[n].astype(f32)

    each(0, 8, collect)
    gi_out[...] = gsum[...].astype(bf16)

    for g in range(GROUPS):
        for i in range(3):
            x_back(g, i).wait_send()
        for q in range(4):
            core_back(g, q, k).wait_send()

    def drain(n):
        spread(bi, bis, bir, n).wait_send()
        spread(go, gos, gor, n).wait_send()
        term(n).wait_send()

    each(0, 8, drain)
    dwout_cp.wait()
    dwin_cp.wait()


def local(block_in, block_out, hidden_pre, w_in, w_out, phrases, region_ids, positive_phrase):
    dma = pltpu.SemaphoreType.DMA
    vm = pltpu.VMEM
    vspec = pl.BlockSpec(memory_space=pltpu.VMEM)
    hspec = pl.BlockSpec(memory_space=pltpu.HBM)
    gi, dwin, dwout = pl.pallas_call(
        kernel,
        out_shape=(
            jax.ShapeDtypeStruct((BLK, DL), bf16),
            jax.ShapeDtypeStruct((DL, FL), bf16),
            jax.ShapeDtypeStruct((FL, DL), bf16),
        ),
        in_specs=[vspec] * 2 + [hspec] * 6,
        out_specs=(vspec, hspec, hspec),
        scratch_shapes=[
            vm((BLK, DL), bf16),
            vm((512, DL), bf16),
            vm((4 * BLK, DL), bf16),
            vm((5, BLK, 128), f32),
            vm((5, 16, 128), f32),
            vm((4, 2, 16, 128), f32),
            vm((7, 2, 16, 128), f32),
            vm((2, 16, 128), f32),
            vm((2, 4, 2, 16, 128), f32),
            vm((4, 4, 2, BLK, DL), bf16),
            vm((4, 4, 2, BLK, DL), bf16),
            vm((DL, FL), bf16),
            vm((FL, DL), bf16),
            vm((4, 4, 2, BLK, FL), bf16),
            vm((4, 4, 2, BLK, FL), bf16),
            vm((8, BLK, FH), f32),
            vm((FL, DL), f32),
            vm((2, DL, FH), f32),
            vm((FL, DL), bf16),
            vm((DL, FL), bf16),
            vm((4, 4, 2, BLK, FH), bf16),
            vm((4, 4, 2, BLK, FH), f32),
            vm((4, 4, 2, BLK, FH), bf16),
            vm((4, 2, BLK, FH), f32),
            vm((12, 2, BLK, FH), bf16),
            vm((12, 2, BLK, FH), bf16),
            vm((4, 2, BLK, FH), bf16),
            vm((4, 2, BLK, FH), bf16),
            vm((2, 4, 4, 2, BLK, FH), bf16),
            vm((4, 4, 2, BLK, DL), bf16),
            vm((32, BLK, DL), bf16),
            vm((BLK, DL), f32),
            dma((13,)), dma((2,)), dma((2,)), dma((2,)), dma, dma, dma((7,)), dma((7,)), dma((7,)), dma((7,)),
            dma((32,)), dma((32,)), dma((32,)), dma((32,)), dma((4,)), dma((4,)), dma((12,)), dma((12,)), dma((4,)), dma((4,)),
            dma((12,)), dma((12,)), dma((16,)), dma((16,)), dma((32,)), dma((32,)),
        ],
        compiler_params=pltpu.CompilerParams(
            collective_id=0, has_side_effects=True, vmem_limit_bytes=60 * 2**20
        ),
        name="mlp_backward",
    )(
        region_ids.reshape(8, 128),
        positive_phrase.reshape(4, 128),
        block_in,
        block_out,
        phrases,
        hidden_pre.reshape(8, 4, BLK, FL),
        w_in,
        w_out,
    )
    return gi, dwin, dwout


def solution(mesh):
    in_specs = (
        P("col", "row"),
        P("col", "row"),
        P(None, "col"),
        P("row", "col"),
        P("col", "row"),
        P(None, "row"),
        P(),
        P(),
    )
    out_specs = (P("col", "row"), P("row", "col"), P("col", "row"))
    return jax.shard_map(local, mesh=mesh, in_specs=in_specs, out_specs=out_specs, check_vma=False)
```

time: 147 us -> 108 us (0.73)
  the two profiles are of different devices: /device:TPU:9 before, /device:TPU:1 now
where the time goes in v2:
time: 108 us; the launch traced here: 107 us
  Pallas kernels  102 us (94%)
  local copies, waits for them, and re-layouts  4.14 us (4%)
    pallas_call x1, Pallas kernels, local(): pl.pallas_call(kernel, out_shape=(jax.ShapeDtypeStruct((BLK, DL), bf16),...  102 us
    unnamed x5, local copies, waits for them, and re-layouts  4.14 us

profile of v2, /device:TPU:1, one launch (start us, length us, event | category | flops | bytes accessed | tf_op | source)
XLA Modules:
  0.0 107.2 jit_solution(376174834094055760)
XLA Ops:
  0.6 102.4 %mlp_backward.1 = (bf16[32,384]{1,0:T(8,128)(2,1)}, bf16[384,768]{1,0:T(8,128)(2,1)}, bf16[768,384]{1,0:T(8,128)(2,1)}) custom-call(s32[8,128]{1,0:T(8,128)} %bitcast.4, s32[4,128]{1,0:T(4,128)} %bitcast.5, bf16[32,384]{1,0:T(8,128)(2,1)} %bi_own.1, bf16[32,384]{1,0:T(8,128)(2,1)} %bo_hbm.1, bf16[512,384]{1,0:T(8,128)(2,1)} %ph_hbm.1, ...), custom_call_target="tpu_custom_call" | custom-call | tf_op jit(solution)/shard_map/mlp_backward/pallas_call | solution.py:387
  103.1 0.0 copy-start
  103.1 1.4 %copy.14 = bf16[32,384]{1,0:T(8,128)(2,1)} copy(bf16[32,384]{1,0:T(8,128)(2,1)} %get-tuple-element.6) | data formatting | bytes 49152
  104.5 1.9 %copy.15 = bf16[384,768]{1,0:T(8,128)(2,1)} copy(bf16[384,768]{1,0:T(8,128)(2,1)} %get-tuple-element.7) | data formatting | bytes 1179648
  106.4 0.0 copy-done
  106.4 0.8 copy.16
Async XLA Ops:
  103.1 3.3 %copy-start = (bf16[768,384]{1,0:T(8,128)(2,1)S(1)}, bf16[768,384]{1,0:T(8,128)(2,1)}, u32[]{:S(2)}) copy-start(bf16[768,384]{1,0:T(8,128)(2,1)} %get-tuple-element.8) | copy-start | bytes 1769476

commit v3 on v2

--- a/solution.py
+++ b/solution.py
@@ -21,10 +21,14 @@
 
 
 GROUPS = 4
-
-
-def away(place):
-    return (place % 2) * ((place + 1) // 2) + (1 - place % 2) * (8 - place // 2)
+AWAY = (1, 7, 0, 4, 3, 5, 2, 6)
+HOME = AWAY.index(0)
+FAR = [AWAY.index(d) for d in (4, 3, 5)]
+NEAR = [AWAY.index(d) for d in (1, 7, 2, 6)]
+
+
+def at(buf, place, part):
+    return buf.at[place // 2, part, place % 2]
 
 
 def nt(a, b):
@@ -53,7 +57,7 @@
     bo_own, ph, ext, part, corebuf, xs, xr, tot, ag,
     go, bi, win, wout, hv, act, slope, dwout, dwin, dwout_b, dwin_b, pact, pown, pcore, acc, pxs, pxr, ysend, yrecv, gh, pbr, rbuf, gsum,
     lsem, osem, halo_s, halo_r, cs, cr, h7s, h7r, a7s, a7r,
-    bis, bir, gos, gor, pcs, pcr, pxss, pxsr, yss, ysr, gxs, gxr, gcs, gcr, rs, rr,
+    bis, bir, brs, brr, gos, gor, fas, far, nes, ner, pcs, pcr, pxss, pxsr, yss, ysr, gxs, gxr, gcs, gcr, rs, rr,
 ):
     r = lax.axis_index("row")
     c = lax.axis_index("col")
@@ -76,12 +80,12 @@
     loads = [
         pltpu.make_async_copy(src, dst, lsem.at[n])
         for n, (src, dst) in enumerate(
-            ((bo_hbm, bo_own), (bi_own, bi.at[0, yl, 0]), (ph_hbm, ph), (wout_hbm, wout), (win_hbm, win))
+            ((bo_hbm, bo_own), (bi_own, at(bi, HOME, yl)), (ph_hbm, ph), (wout_hbm, wout), (win_hbm, win))
         )
     ]
     loads += [
         pltpu.make_async_copy(
-            h_hbm.at[(z + away(p)) % 8], hv.at[p // 2, :, p % 2], lsem.at[5 + p]
+            h_hbm.at[(z + AWAY[p]) % 8], hv.at[p // 2, :, p % 2], lsem.at[5 + p]
         )
         for p in range(8)
     ]
@@ -114,27 +118,50 @@
     ext[pl.ds(BLK, BLK), :] = bo_own[...]
     ext[pl.ds(3 * BLK, BLK), :] = jnp.zeros((BLK, DL), bf16)
 
-    def spread(buf, send, recv, n):
-        place, to = n // 4, n % 4
-        dev = cdev(((z + 8 - away(place)) % 8) * 4 + to)
-        return rcopy(buf.at[0, yl, 0], buf.at[place // 2, yl, place % 2], send.at[n], recv.at[place * 4 + yl], dev)
-
-    def landed(buf, send, recv, n):
-        place, of = n // 4, n % 4
-        slot = buf.at[place // 2, of, place % 2]
-        return rcopy(slot, slot, send.at[n], recv.at[n], cdev(((z + away(place)) % 8) * 4 + of))
-
-    def each(lo, hi, step):
-        def body(n, _):
-            @pl.when(n != yl)
-            def _():
-                step(n)
-
-            return 0
-
-        lax.fori_loop(4 * lo, 4 * hi, body, 0)
-
-    each(0, 8, lambda n: spread(bi, bis, bir, n).start())
+    def spread(buf, send, recv, place, to):
+        n = place * 4 + to
+        slot = at(buf, place, yl)
+        return rcopy(slot, slot, send.at[n], recv.at[place * 4 + yl], cdev(z * 4 + to))
+
+    def landed(buf, send, recv, place, of):
+        n = place * 4 + of
+        slot = at(buf, place, of)
+        return rcopy(slot, slot, send.at[n], recv.at[n], cdev(z * 4 + of))
+
+    def each(places, step, every=False):
+        for place in places:
+
+            def body(n, _):
+                if every:
+                    step(place, n)
+                else:
+
+                    @pl.when(n != yl)
+                    def _():
+                        step(place, n)
+
+                return 0
+
+            lax.fori_loop(0, 4, body, 0)
+
+    def ring(step, back):
+        src = AWAY.index(((step - 1) * (7 - 6 * back)) % 8)
+        dst = AWAY.index((step * (7 - 6 * back)) % 8)
+        half = pl.ds(0, 4) if step < 4 else pl.ds(2 * back, 2)
+        n = 2 * step + back
+        to = cdev(((z + 1 + 6 * back) % 8) * 4 + yl)
+        return rcopy(at(bi, src, half), at(bi, dst, half), brs.at[n - 2], brr.at[n - 2], to)
+
+    def ring_step(step):
+        if step == 1:
+            each((HOME,), lambda p, n: landed(bi, bis, bir, p, n).wait_recv())
+        for back in range(2):
+            if step > 1:
+                ring(step - 1, back).wait_recv()
+            if step < 5:
+                ring(step, back).start()
+
+    each((HOME,), lambda p, n: spread(bi, bis, bir, p, n).start())
 
     lane = lax.broadcasted_iota(jnp.int32, (BLK, 128), 1)
     sub = lax.broadcasted_iota(jnp.int32, (BLK, 128), 0)
@@ -165,6 +192,8 @@
     for j in range(4):
         part[j] = inner[:, j * 128 : (j + 1) * 128]
     part[4] = jnp.broadcast_to(squares, (BLK, 128))
+
+    ring_step(1)
 
     mine = pl.ds(pl.multiple_of(k * 16, 16), 16)
     theirs = pl.ds(pl.multiple_of(ko * 16, 16), 16)
@@ -192,6 +221,7 @@
         return 0
 
     lax.fori_loop(0, 16, act_step, 0)
+    ring_step(2)
 
     for cp in sends:
         cp.wait()
@@ -216,6 +246,7 @@
         return 0
 
     lax.fori_loop(0, 8, slope_step, 0)
+    ring_step(3)
 
     for cp in sends:
         cp.wait()
@@ -234,9 +265,33 @@
     pulled = pulled3[:BLK] + (pulled3[BLK : 2 * BLK] + pulled3[2 * BLK :])
     curve = jnp.sum(grads * scores, axis=1, keepdims=True)
     grad_pooled = pulled / norms - curve * pooled / (width * norms * norms)
-    go[0, yl, 0] = (grad_pooled / counts).astype(bf16)
-
-    each(0, 8, lambda n: spread(go, gos, gor, n).start())
+    go[HOME // 2, yl, HOME % 2] = (grad_pooled / counts).astype(bf16)
+
+    def to_far(n):
+        place = FAR[n]
+        dev = cdev(((z + 8 - AWAY[place]) % 8) * 4 + yl)
+        return rcopy(at(go, HOME, yl), at(go, place, yl), fas.at[n], far.at[n], dev)
+
+    def to_near(n):
+        place = NEAR[n]
+        dev = cdev(((z + 8 - AWAY[place]) % 8) * 4 + yl)
+        return rcopy(at(go, HOME, pl.ds(0, 4)), at(go, place, pl.ds(0, 4)), nes.at[n], ner.at[n], dev)
+
+    def go_landed(places):
+        each(places, lambda p, n: landed(go, gos, gor, p, n).wait_recv())
+
+    def go_spread(places):
+        each(places, lambda p, n: spread(go, gos, gor, p, n).start())
+
+    go_spread((HOME,))
+    for n in range(3):
+        to_far(n).start()
+    go_landed((HOME,))
+    for n in range(4):
+        to_near(n).start()
+    for n in range(3):
+        to_far(n).wait_recv()
+        go_spread(FAR[n : n + 1])
 
     for cp in loads[3:5]:
         cp.wait()
@@ -265,13 +320,21 @@
         slot = gh.at[kk, g, q]
         return rcopy(slot, slot, gcs.at[g * 4 + q], gcr.at[g * 4 + q], rdev(x, yh, ko))
 
-    def term(n):
-        place, to = n // 4, n % 4
-        dev = cdev(((z + away(place)) % 8) * 4 + to)
-        return rcopy(pbr.at[place // 2, to, place % 2], rbuf.at[place * 4 + yl], rs.at[n], rr.at[place * 4 + yl], dev)
+    def term(place, to):
+        n = place * 4
+        dev = cdev(((z + AWAY[place]) % 8) * 4 + to)
+        return rcopy(at(pbr, place, to), rbuf.at[n + yl], rs.at[n + to], rr.at[n + yl], dev)
+
+    def terms(places, step):
+        for place in places:
+            each((place,), step, every=place != HOME)
 
     def product(g):
-        each(2 * g, 2 * g + 2, lambda n: landed(go, gos, gor, n).wait_recv())
+        for place in (2 * g, 2 * g + 1):
+            if place in NEAR:
+                to_near(NEAR.index(place)).wait_recv()
+            elif place in FAR:
+                go_landed((place,))
         a = go[g].reshape(8 * BLK, DL)
         pact[g] = nt(a, whalf[0][...]).astype(bf16).reshape(4, 2, BLK, FH)
         core_sum(g).start()
@@ -313,7 +376,7 @@
             core_back(g, q, ko).wait_recv()
         val = nt(gh[0, g].reshape(8 * BLK, FH), win[:, :FH]) + nt(gh[1, g].reshape(8 * BLK, FH), win[:, FH:])
         pbr[g] = val.astype(bf16).reshape(4, 2, BLK, DL)
-        each(2 * g, 2 * g + 2, lambda n: term(n).start())
+        terms((2 * g, 2 * g + 1), lambda p, n: term(p, n).start())
 
     def weight_out(g):
         val = tn(act[g].reshape(8 * BLK, FL), go[g].reshape(8 * BLK, DL))
@@ -348,19 +411,22 @@
                 step(g)
         if 0 <= t - 1 < GROUPS:
             weight_out(t - 1)
+        if t == 1:
+            ring_step(4)
         if t == GROUPS:
-            each(0, 8, lambda n: landed(bi, bis, bir, n).wait_recv())
+            ring_step(5)
         if 0 <= t - 5 < GROUPS:
             weight_in(t - 5)
 
-    gsum[...] = go[0, yl, 0].astype(f32) + pbr[0, yl, 0].astype(f32)
-
-    def collect(n):
+    gsum[...] = go[HOME // 2, yl, HOME % 2].astype(f32) + pbr[HOME // 2, yl, HOME % 2].astype(f32)
+
+    def collect(place, of):
+        n = place * 4 + of
         slot = rbuf.at[n]
         rcopy(slot, slot, rs.at[n], rr.at[n], cdev((c + 1) % 32)).wait_recv()
         gsum[...] += rbuf[n].astype(f32)
 
-    each(0, 8, collect)
+    terms(range(8), collect)
     gi_out[...] = gsum[...].astype(bf16)
 
     for g in range(GROUPS):
@@ -369,12 +435,16 @@
         for q in range(4):
             core_back(g, q, k).wait_send()
 
-    def drain(n):
-        spread(bi, bis, bir, n).wait_send()
-        spread(go, gos, gor, n).wait_send()
-        term(n).wait_send()
-
-    each(0, 8, drain)
+    terms(range(8), lambda p, n: term(p, n).wait_send())
+    each([HOME] + FAR, lambda p, n: spread(go, gos, gor, p, n).wait_send())
+    for n in range(3):
+        to_far(n).wait_send()
+    for n in range(4):
+        to_near(n).wait_send()
+    each((HOME,), lambda p, n: spread(bi, bis, bir, p, n).wait_send())
+    for step in range(1, 5):
+        for back in range(2):
+            ring(step, back).wait_send()
     dwout_cp.wait()
     dwin_cp.wait()
 
@@ -427,7 +497,8 @@
             vm((32, BLK, DL), bf16),
             vm((BLK, DL), f32),
             dma((13,)), dma((2,)), dma((2,)), dma((2,)), dma, dma, dma((7,)), dma((7,)), dma((7,)), dma((7,)),
-            dma((32,)), dma((32,)), dma((32,)), dma((32,)), dma((4,)), dma((4,)), dma((12,)), dma((12,)), dma((4,)), dma((4,)),
+            dma((32,)), dma((32,)), dma((8,)), dma((8,)), dma((32,)), dma((32,)), dma((3,)), dma((3,)), dma((4,)), dma((4,)),
+            dma((4,)), dma((4,)), dma((12,)), dma((12,)), dma((4,)), dma((4,)),
             dma((12,)), dma((12,)), dma((16,)), dma((16,)), dma((32,)), dma((32,)),
         ],
         compiler_params=pltpu.CompilerParams(

time: 108 us -> 98.3 us (0.910)
  Pallas kernels: 102 us -> 93.3 us
    pallas_call x1, Pallas kernels: 102 us -> 93.3 us  [local(): pl.pallas_call(kernel, out_shape=(jax.ShapeDtypeStruct((BLK, DL), bf16),...]
where the time goes in v3:
time: 98.3 us; the launch traced here: 98.1 us
  Pallas kernels  93.3 us (95%)
  local copies, waits for them, and re-layouts  4.14 us (4%)
    pallas_call x1, Pallas kernels, local(): pl.pallas_call(kernel, out_shape=(jax.ShapeDtypeStruct((BLK, DL), bf16),...  93.3 us
    unnamed x5, local copies, waits for them, and re-layouts  4.14 us

profile of v3, /device:TPU:1, one launch (start us, length us, event | category | flops | bytes accessed | tf_op | source)
XLA Modules:
  0.0 98.1 jit_solution(16333934457453912238)
XLA Ops:
  0.6 93.3 %mlp_backward.1 = (bf16[32,384]{1,0:T(8,128)(2,1)}, bf16[384,768]{1,0:T(8,128)(2,1)}, bf16[768,384]{1,0:T(8,128)(2,1)}) custom-call(s32[8,128]{1,0:T(8,128)} %bitcast.4, s32[4,128]{1,0:T(4,128)} %bitcast.5, bf16[32,384]{1,0:T(8,128)(2,1)} %bi_own.1, bf16[32,384]{1,0:T(8,128)(2,1)} %bo_hbm.1, bf16[512,384]{1,0:T(8,128)(2,1)} %ph_hbm.1, ...), custom_call_target="tpu_custom_call" | custom-call | tf_op jit(solution)/shard_map/mlp_backward/pallas_call | solution.py:457
  94.0 0.0 copy-start
  94.0 1.4 %copy.14 = bf16[32,384]{1,0:T(8,128)(2,1)} copy(bf16[32,384]{1,0:T(8,128)(2,1)} %get-tuple-element.6) | data formatting | bytes 49152
  95.4 1.9 %copy.15 = bf16[384,768]{1,0:T(8,128)(2,1)} copy(bf16[384,768]{1,0:T(8,128)(2,1)} %get-tuple-element.7) | data formatting | bytes 1179648
  97.3 0.0 copy-done
  97.3 0.8 copy.16
Async XLA Ops:
  94.0 3.3 %copy-start = (bf16[768,384]{1,0:T(8,128)(2,1)S(1)}, bf16[768,384]{1,0:T(8,128)(2,1)}, u32[]{:S(2)}) copy-start(bf16[768,384]{1,0:T(8,128)(2,1)} %get-tuple-element.8) | copy-start | bytes 1769476

commit v4 on v3

--- a/solution.py
+++ b/solution.py
@@ -21,7 +21,7 @@
 
 
 GROUPS = 4
-AWAY = (1, 7, 0, 4, 3, 5, 2, 6)
+AWAY = (0, 4, 3, 5, 2, 6, 1, 7)
 HOME = AWAY.index(0)
 FAR = [AWAY.index(d) for d in (4, 3, 5)]
 NEAR = [AWAY.index(d) for d in (1, 7, 2, 6)]
@@ -131,7 +131,8 @@
     def each(places, step, every=False):
         for place in places:
 
-            def body(n, _):
+            def body(m, _):
+                n = (yl + m) % 4
                 if every:
                     step(place, n)
                 else:

time: 98.3 us -> 97.1 us (0.988)
  Pallas kernels: 93.3 us -> 92.1 us
    pallas_call x1, Pallas kernels: 93.3 us -> 92.1 us  [local(): pl.pallas_call(kernel, out_shape=(jax.ShapeDtypeStruct((BLK, DL), bf16),...]
where the time goes in v4:
time: 97.1 us; the launch traced here: 96.8 us
  Pallas kernels  92.1 us (95%)
  local copies, waits for them, and re-layouts  4.14 us (4%)
    pallas_call x1, Pallas kernels, local(): pl.pallas_call(kernel, out_shape=(jax.ShapeDtypeStruct((BLK, DL), bf16),...  92.1 us
    unnamed x5, local copies, waits for them, and re-layouts  4.14 us

profile of v4, /device:TPU:1, one launch (start us, length us, event | category | flops | bytes accessed | tf_op | source)
XLA Modules:
  0.0 96.8 jit_solution(3972333810081056610)
XLA Ops:
  0.6 92.1 %mlp_backward.1 = (bf16[32,384]{1,0:T(8,128)(2,1)}, bf16[384,768]{1,0:T(8,128)(2,1)}, bf16[768,384]{1,0:T(8,128)(2,1)}) custom-call(s32[8,128]{1,0:T(8,128)} %bitcast.4, s32[4,128]{1,0:T(4,128)} %bitcast.5, bf16[32,384]{1,0:T(8,128)(2,1)} %bi_own.1, bf16[32,384]{1,0:T(8,128)(2,1)} %bo_hbm.1, bf16[512,384]{1,0:T(8,128)(2,1)} %ph_hbm.1, ...), custom_call_target="tpu_custom_call" | custom-call | tf_op jit(solution)/shard_map/mlp_backward/pallas_call | solution.py:458
  92.7 0.0 copy-start
  92.7 1.4 %copy.14 = bf16[32,384]{1,0:T(8,128)(2,1)} copy(bf16[32,384]{1,0:T(8,128)(2,1)} %get-tuple-element.6) | data formatting | bytes 49152
  94.1 1.9 %copy.15 = bf16[384,768]{1,0:T(8,128)(2,1)} copy(bf16[384,768]{1,0:T(8,128)(2,1)} %get-tuple-element.7) | data formatting | bytes 1179648
  96.0 0.0 copy-done
  96.0 0.8 copy.16
Async XLA Ops:
  92.7 3.3 %copy-start = (bf16[768,384]{1,0:T(8,128)(2,1)S(1)}, bf16[768,384]{1,0:T(8,128)(2,1)}, u32[]{:S(2)}) copy-start(bf16[768,384]{1,0:T(8,128)(2,1)} %get-tuple-element.8) | copy-start | bytes 1769476

commit v5 on v4

--- a/solution.py
+++ b/solution.py
@@ -21,10 +21,10 @@
 
 
 GROUPS = 4
-AWAY = (0, 4, 3, 5, 2, 6, 1, 7)
+AWAY = (0, 4, 2, 6, 3, 5, 1, 7)
 HOME = AWAY.index(0)
 FAR = [AWAY.index(d) for d in (4, 3, 5)]
-NEAR = [AWAY.index(d) for d in (1, 7, 2, 6)]
+NEAR = [AWAY.index(d) for d in (2, 6, 1, 7)]
 
 
 def at(buf, place, part):

time: 97.1 us -> 97 us (level)
  no operation moved by 1% of the time
where the time goes in v5:
time: 97 us; the launch traced here: 96.8 us
  Pallas kernels  92 us (95%)
  local copies, waits for them, and re-layouts  4.14 us (4%)
    pallas_call x1, Pallas kernels, local(): pl.pallas_call(kernel, out_shape=(jax.ShapeDtypeStruct((BLK, DL), bf16),...  92 us
    unnamed x5, local copies, waits for them, and re-layouts  4.14 us

profile of v5, /device:TPU:1, one launch (start us, length us, event | category | flops | bytes accessed | tf_op | source)
XLA Modules:
  0.0 96.8 jit_solution(6161191325334819774)
XLA Ops:
  0.6 92.0 %mlp_backward.1 = (bf16[32,384]{1,0:T(8,128)(2,1)}, bf16[384,768]{1,0:T(8,128)(2,1)}, bf16[768,384]{1,0:T(8,128)(2,1)}) custom-call(s32[8,128]{1,0:T(8,128)} %bitcast.4, s32[4,128]{1,0:T(4,128)} %bitcast.5, bf16[32,384]{1,0:T(8,128)(2,1)} %bi_own.1, bf16[32,384]{1,0:T(8,128)(2,1)} %bo_hbm.1, bf16[512,384]{1,0:T(8,128)(2,1)} %ph_hbm.1, ...), custom_call_target="tpu_custom_call" | custom-call | tf_op jit(solution)/shard_map/mlp_backward/pallas_call | solution.py:458
  92.7 0.0 copy-start
  92.7 1.4 %copy.14 = bf16[32,384]{1,0:T(8,128)(2,1)} copy(bf16[32,384]{1,0:T(8,128)(2,1)} %get-tuple-element.6) | data formatting | bytes 49152
  94.1 1.9 %copy.15 = bf16[384,768]{1,0:T(8,128)(2,1)} copy(bf16[384,768]{1,0:T(8,128)(2,1)} %get-tuple-element.7) | data formatting | bytes 1179648
  96.0 0.0 copy-done
  96.0 0.8 copy.16
Async XLA Ops:
  92.7 3.3 %copy-start = (bf16[768,384]{1,0:T(8,128)(2,1)S(1)}, bf16[768,384]{1,0:T(8,128)(2,1)}, u32[]{:S(2)}) copy-start(bf16[768,384]{1,0:T(8,128)(2,1)} %get-tuple-element.8) | copy-start | bytes 1769476
